TPU v7x, 32 devices: a whole 2x2x4 slice. The times are simulated.
32 devices in a mesh: pool: 4 (over y, x), section: 2 (over core), tensor: 4 (over z).
Axes of the slice: x: 2, y: 2, z: 4, core: 2. Of those that a mesh axis runs over, the one named last changes fastest.
Arguments:
- hidden_input: bfloat16 [2048, 8192], P('pool', 'tensor'), may hold values from -6 to 6
- attention_output: bfloat16 [2, 2048, 8192], P('section', 'pool', 'tensor'), may hold values from -6 to 6
- projection_weight: bfloat16 [2, 8192, 8192], P('section', 'tensor'), may hold values from -0.09375 to 0.09375
- lowrank_down_factor: bfloat16 [2, 128, 64, 8192], P('section', 'pool', None, 'tensor'), may hold values from -0.0625 to 0.0625
- lowrank_up_factor: bfloat16 [2, 128, 64, 8192], P('section', 'pool', None, 'tensor'), may hold values from -0.75 to 0.75
- residual_block_mats: bfloat16 [2, 128, 4, 128, 128], P('section', 'pool', 'tensor'), may hold values from -0.5 to 0.5
- diagonal_block_index: int32 [2, 128, 4], P('section', 'pool', 'tensor'), may hold values from 0 to 63, as said below
- row_variant_index: int32 [2048], P('pool'), may hold values from 0 to 127, as said below
Outputs:
- hidden_out: bfloat16 [2, 2048, 8192], P('section', 'pool', 'tensor')
Inputs may be any that keep to these rules, and one draw needn't show every extreme that they name: `row_variant_index`: within each aligned block of 512 rows the ids never fall; at most 256 rows of a block name variants of one owner q (ids q * 32 to (q + 1) * 32 - 1), and some owner receives exactly 256 rows from every block. `diagonal_block_index`: entry j of each list lies in j * 16 to (j + 1) * 16 - 1.
All inputs are finite; a program needn't handle non-finite values.
Results may differ from a plain program's by a relative error of at most 0.017.
Values may be sent and summed in bfloat16 or wider, within the bound.
A program may use at most 128 MiB of HBM per device.

v0:
```python
import jax
import jax.numpy as jnp
from jax import lax
from jax.sharding import PartitionSpec as P


def shifted(value, axis, steps):
    count = lax.axis_size(axis)
    first, last = (max(0, -steps), min(count, count - steps))
    return lax.ppermute(value, axis, [(source, source + steps) for source in range(first, last)])


def adapter_delta(
    features, select, down_factor_rows, up_factor_rows, block_mats, place_hot, reducer
):
    var_count, low_dim, shard_width = down_factor_rows.shape
    block_size = block_mats.shape[-1]
    per_shard = shard_width // block_size
    projected = lax.dot_general(
        features,
        down_factor_rows.reshape(var_count * low_dim, shard_width),
        (((1,), (1,)), ((), ())),
        preferred_element_type=jnp.float32,
    )
    partial_value = jnp.einsum("svr,sv->sr", projected.reshape(-1, var_count, low_dim), select)
    lowrank_product = reducer(partial_value).astype(jnp.bfloat16)
    spread = (select.astype(jnp.bfloat16)[:, :, None] * lowrank_product[:, None, :]).reshape(
        -1, var_count * low_dim
    )
    lowrank_output = jnp.dot(
        spread,
        up_factor_rows.reshape(var_count * low_dim, shard_width),
        preferred_element_type=jnp.float32,
    )
    row_place = jnp.dot(select, place_hot.astype(jnp.float32))
    feat_blocks = features.reshape(-1, per_shard, block_size)
    picked = jnp.sum(feat_blocks * row_place.astype(jnp.bfloat16)[:, :, None], axis=1)
    stacked = jnp.transpose(block_mats, (1, 0, 2)).reshape(block_size, var_count * block_size)
    block_y = jnp.dot(picked, stacked, preferred_element_type=jnp.float32).reshape(
        -1, var_count, block_size
    )
    block_sel = jnp.einsum("svj,sv->sj", block_y, select)
    block_output = (row_place[:, :, None] * block_sel[:, None, :]).reshape(-1, shard_width)
    return (lowrank_output + block_output).astype(jnp.bfloat16)


def per_device(
    hidden_input,
    attention_output,
    projection_weight,
    lowrank_down_factor,
    lowrank_up_factor,
    residual_block_mats,
    diagonal_block_index,
    row_variant_index,
):
    features = attention_output[0]
    weight = projection_weight[0]
    row_count_dev, shard_width = features.shape
    down_factor_rows = lowrank_down_factor[0]
    up_factor_rows = lowrank_up_factor[0]
    block_mats = residual_block_mats[0][:, 0]
    var_count = down_factor_rows.shape[0]
    block_size = block_mats.shape[-1]
    per_shard = shard_width // block_size
    tensor_pos = lax.axis_index("tensor")
    section_pos = lax.axis_index("section")
    place_hot = (
        (diagonal_block_index[0][:, 0] - tensor_pos * per_shard)[:, None]
        == jnp.arange(per_shard)[None, :]
    ).astype(jnp.bfloat16)
    base_sum = lax.psum_scatter(
        lax.dot_general(
            weight, features, (((0,), (1,)), ((), ())), preferred_element_type=jnp.float32
        ).astype(jnp.bfloat16),
        "tensor",
        scatter_dimension=0,
        tiled=True,
    ).astype(jnp.float32)
    pool_count = lax.axis_size("pool")
    capacity = row_count_dev // 2
    owners = row_variant_index // var_count
    owner_hot = (owners[:, None] == jnp.arange(pool_count)[None, :]).astype(jnp.int32)
    counts = jnp.sum(owner_hot, axis=0)
    starts = jnp.cumsum(counts) - counts
    slot_pos = jnp.arange(row_count_dev) - jnp.sum(owner_hot * starts[None, :], axis=1)
    filled = jnp.arange(capacity)[None, :] < counts[:, None]
    source = jnp.minimum(starts[:, None] + jnp.arange(capacity)[None, :], row_count_dev - 1)
    send_feat = jnp.where(
        filled[:, :, None], jnp.take(features, source, axis=0), jnp.zeros((), jnp.bfloat16)
    )
    send_var = jnp.where(
        filled,
        jnp.take(row_variant_index, source) - jnp.arange(pool_count)[:, None] * var_count,
        -1,
    ).astype(jnp.bfloat16)
    recv_feat = lax.all_to_all(send_feat, "pool", split_axis=0, concat_axis=0, tiled=True)
    recv_var = lax.all_to_all(send_var, "pool", split_axis=0, concat_axis=0, tiled=True)
    group_count, item_count = recv_var.shape
    flat_var = recv_var.reshape(group_count * item_count)
    select = (flat_var[:, None] == jnp.arange(var_count).astype(jnp.bfloat16)[None, :]).astype(
        jnp.float32
    )

    def slot_reduce(partial_value):
        return lax.psum(partial_value.astype(jnp.bfloat16), "tensor").astype(jnp.float32)

    served = adapter_delta(
        recv_feat.reshape(group_count * item_count, shard_width),
        select,
        down_factor_rows,
        up_factor_rows,
        block_mats,
        place_hot,
        slot_reduce,
    )
    returned = lax.all_to_all(
        served.reshape(group_count, item_count, shard_width),
        "pool",
        split_axis=0,
        concat_axis=0,
        tiled=True,
    )
    flat_back = returned.reshape(pool_count * capacity, shard_width)
    adapter_output = jnp.take(flat_back, owners * capacity + slot_pos, axis=0)
    branch = jnp.transpose(base_sum) + adapter_output.astype(jnp.float32)
    first_out = (hidden_input.astype(jnp.float32) + branch).astype(jnp.bfloat16)
    carried = shifted(first_out, "section", 1)
    start_rows = jnp.where(section_pos == 0, hidden_input, carried)
    return (start_rows.astype(jnp.float32) + branch).astype(jnp.bfloat16)[None]


def solution(mesh):
    return jax.shard_map(
        per_device,
        mesh=mesh,
        in_specs=(
            P("pool", "tensor"),
            P("section", "pool", "tensor"),
            P("section", "tensor", None),
            P("section", "pool", None, "tensor"),
            P("section", "pool", None, "tensor"),
            P("section", "pool", "tensor", None, None),
            P("section", "pool", "tensor"),
            P("pool"),
        ),
        out_specs=P("section", "pool", "tensor"),
        check_vma=False,
    )
```

profile of v0, /device:TPU:17, one launch (start us, length us, event | category | flops | bytes accessed | tf_op | source)
XLA Modules:
  0.0 304.9 jit_solution(596026224294542796)
XLA Ops:
  6.5 0.0 copy-start
  6.5 0.8 add_select_fusion
  7.4 0.1 convert_reduce_fusion
  7.5 0.2 reduce-window.7
  7.7 0.1 fusion.23
  7.8 6.2 %gather_fusion = s32[1024]{0:T(1024)S(1)} fusion(s32[512]{0:T(512)} %param.15, s32[1024]{0:T(1024)S(1)} %broadcast_clamp_fusion), kind=kCustom, calls=%fused_computation | custom fusion | bytes 12288 | tf_op jit(solution)/shard_map/jit(_take)/gather | solution.py:94
  14.0 0.1 fusion.24
  14.1 0.5 broadcast.262
  14.6 0.7 reduce.4
  15.2 0.6 reshape.351
  15.8 3.4 %all-to-all-start = ((bf16[4,2,128]{2,1,0:T(2,128)(2,1)}), bf16[4,2,128]{2,1,0:T(2,128)(2,1)S(1)}, u32[]{:S(2)}, u32[]{:S(2)}) async-start(bf16[4,2,128]{2,1,0:T(2,128)(2,1)} %reshape.351), calls=%async_computation.1 | async-start | bytes 4096 | tf_op jit(solution)/shard_map/all_to_all | solution.py:98
  19.3 0.1 compare_and_fusion
  19.3 0.1 iota_compare_fusion.3
  19.4 0.0 copy-done
  19.4 6.0 %gather_fusion.1 = bf16[1024,2048]{1,0:T(8,128)(2,1)} fusion(bf16[512,2048]{1,0:T(8,128)(2,1)S(1)} %bitcast.76, s32[1024]{0:T(1024)S(1)} %broadcast_clamp_fusion), kind=kCustom, calls=%fused_computation.1 | custom fusion | bytes 8392704 | tf_op jit(solution)/shard_map/jit(_take)/gather | solution.py:90
  25.4 3.9 %select_select_fusion = bf16[4,256,2048]{2,1,0:T(8,128)(2,1)} fusion(bf16[4,256,2048]{2,1,0:T(8,128)(2,1)} %bitcast.77, pred[4,256]{1,0:T(4,128)(4,1)S(1)} %compare_and_fusion, pred[4,256]{1,0:T(4,128)(4,1)S(1)} %iota_compare_fusion.3), kind=kLoop, calls=%fused_computation.19 | loop fusion | flops 4194304 | bytes 8390656 | tf_op jit(solution)/shard_map/jit(_where)/select_n | solution.py:89
  29.3 0.0 all-to-all-done
  29.3 4.9 %all-to-all-start.1 = ((bf16[4,256,2048]{2,1,0:T(8,128)(2,1)}), bf16[4,256,2048]{2,1,0:T(8,128)(2,1)}, u32[]{:S(2)}, u32[]{:S(2)}) async-start(bf16[4,256,2048]{2,1,0:T(8,128)(2,1)} %select_select_fusion), calls=%async_computation.2 | async-start | bytes 8388608 | tf_op jit(solution)/shard_map/all_to_all | solution.py:97
  34.3 0.0 all-reduce.2.cloned.1.call-start
  34.4 0.1 fusion.19
  34.5 46.6 %all-to-all-done.1 = bf16[4,256,2048]{2,1,0:T(8,128)(2,1)} async-done(((bf16[4,256,2048]{2,1,0:T(8,128)(2,1)}), bf16[4,256,2048]{2,1,0:T(8,128)(2,1)}, u32[]{:S(2)}, u32[]{:S(2)}) %all-to-all-start.1) | async-done | bytes 4194336 | tf_op jit(solution)/shard_map/all_to_all | solution.py:97
  81.1 13.2 %multiply_reduce_fusion = bf16[1024,64]{0,1:T(8,128)(2,1)} fusion(f32[1024,32]{0,1:T(8,128)S(1)} %get-tuple-element.9, bf16[1024,2048,1]{1,0,2:T(8,128)(2,1)} %bitcast.8, bf16[1,32,64,2048]{3,2,1,0:T(8,128)(2,1)} %param.11), kind=kOutput, calls=%fused_computation.12 | convolution fusion | flops 8594063360 | bytes 12845056 | tf_op jit(solution)/shard_map/dot_general | solution.py:19
  94.4 0.0 all-reduce.2.cloned.1.call-update
  94.4 0.2 reduce-scatter.2.cloned.1.call-start
  94.6 25.7 %fusion.4 = bf16[8192,512]{1,0:T(8,128)(2,1)} fusion(bf16[1,2048,8192]{2,1,0:T(8,128)(2,1)} %param.10, bf16[1,512,2048]{2,1,0:T(8,128)(2,1)S(1)} %copy-done), kind=kOutput, calls=%fused_computation.7 | convolution fusion | flops 17184063488 | bytes 44040192 | tf_op jit(solution)/shard_map/dot_general | solution.py:73
  120.3 0.0 copy-start.4
  120.3 0.0 copy-start.5
  120.3 0.0 reduce-scatter.2.cloned.1.call-update
  120.4 1.2 copy-done.4
  121.6 0.7 copy.32
  122.2 0.0 copy-done.5
  122.2 0.3 fusion.28
  122.5 0.2 copy.31
  122.7 0.9 copy.41
  123.6 0.2 copy.30
  123.8 3.6 %copy.47 = bf16[128,8,16,128]{3,2,1,0:T(8,128)(2,1)S(1)} copy(bf16[128,8,16,128]{3,1,2,0:T(8,128)(2,1)} %bitcast.36) | data formatting | bytes 8388608
  127.4 11.6 %fusion.10 = bf16[1024,128]{1,0:T(8,128)(2,1)S(1)} fusion(bf16[128,8,16,128]{3,2,1,0:T(8,128)(2,1)S(1)} %copy.47, bf16[1024,16]{1,0:T(8,128)(2,1)S(1)} %copy.31), kind=kLoop, calls=%fused_computation.14 | loop fusion | flops 4063232 | bytes 4489216 | tf_op jit(solution)/shard_map/reduce_sum | solution.py:37
  139.0 2.3 fusion.14
  141.3 17.5 %fusion.2 = f32[1024,1,128]{2,1,0:T(1,128)S(1)} fusion(pred[1024,32,1]{1,2,0:T(4,128)(4,1)S(1)} %copy.41, bf16[1024,32,128]{2,0,1:T(8,128)(2,1)S(1)} %fusion.14), kind=kOutput, calls=%fused_computation.5 | convolution fusion | flops 8388608 | bytes 8945664 | tf_op jit(solution)/shard_map/svj,sv->sj/dot_general | solution.py:42
  158.9 7.2 %broadcast_multiply_fusion = f32[1024,16,128]{2,1,0:T(8,128)} fusion(f32[1024,128]{1,0:T(8,128)S(1)} %bitcast.81, f32[1024,16]{1,0:T(8,128)S(1)} %copy.30), kind=kLoop, calls=%fused_computation.18 | loop fusion | flops 2097152 | bytes 8978432 | tf_op jit(solution)/shard_map/mul | solution.py:43
  166.1 0.0 all-reduce.2.cloned.1.call-done
  166.1 1.2 broadcast_multiply_fusion.1
  167.3 18.1 %fusion.7 = bf16[1024,2048]{1,0:T(8,128)(2,1)} fusion(f32[128,8,16,128]{3,2,1,0:T(8,128)} %bitcast.78, bf16[1024,2048]{0,1:T(8,128)(2,1)S(1)} %bitcast.80, bf16[2048,2048]{1,0:T(8,128)(2,1)} %bitcast.88), kind=kOutput, calls=%fused_computation.9 | convolution fusion | flops 8594128896 | bytes 25165824 | tf_op jit(solution)/shard_map/dot_general | solution.py:30
  185.4 4.9 %all-to-all-start.2 = ((bf16[4,256,2048]{2,1,0:T(8,128)(2,1)}), bf16[4,256,2048]{2,1,0:T(8,128)(2,1)}, u32[]{:S(2)}, u32[]{:S(2)}) async-start(bf16[4,256,2048]{2,1,0:T(8,128)(2,1)} %bitcast.79), calls=%async_computation.3 | async-start | bytes 8388608 | tf_op jit(solution)/shard_map/all_to_all | solution.py:117
  190.3 0.0 copy-start.2
  190.3 4.0 %copy.34 = bf16[512,2048]{0,1:T(8,128)(2,1)} copy(bf16[512,2048]{1,0:T(8,128)(2,1)} %param.8) | data formatting | bytes 4194304 | tf_op args[0]
  194.4 0.1 select_reduce_fusion
  194.4 0.0 copy-done.2
  194.5 42.7 %all-to-all-done.2 = bf16[4,256,2048]{2,1,0:T(8,128)(2,1)} async-done(((bf16[4,256,2048]{2,1,0:T(8,128)(2,1)}), bf16[4,256,2048]{2,1,0:T(8,128)(2,1)}, u32[]{:S(2)}, u32[]{:S(2)}) %all-to-all-start.2) | async-done | bytes 4194336 | tf_op jit(solution)/shard_map/all_to_all | solution.py:117
  237.2 8.0 %gather_fusion.2 = bf16[512,2048]{1,0:T(8,128)(2,1)} fusion(bf16[1024,2048]{1,0:T(8,128)(2,1)} %bitcast.23, s32[1024]{0:T(1024)S(1)} %pad_clamp_fusion), kind=kCustom, calls=%fused_computation.2 | custom fusion | bytes 4196352 | tf_op jit(solution)/shard_map/jit(_take)/gather | solution.py:125
  245.1 0.0 copy-start.3
  245.1 4.1 %copy.33 = bf16[512,2048]{0,1:T(8,128)(2,1)} copy(bf16[512,2048]{1,0:T(8,128)(2,1)} %gather_fusion.2) | data formatting | bytes 4194304 | tf_op jit(solution)/shard_map/jit(_take)/gather | solution.py:125
  249.2 28.1 %reduce-scatter.2.cloned.1.call-done = bf16[2048,512]{1,0:T(8,128)(2,1)} async-done(((bf16[8192,512]{1,0:T(8,128)(2,1)}), bf16[2048,512]{1,0:T(8,128)(2,1)}) %reduce-scatter.2.cloned.1.call-update) | async-done | bytes 2097168 | tf_op jit(solution)/shard_map/reduce_scatter | solution.py:72
  277.3 0.0 copy-done.3
  277.3 4.4 %add_convert_fusion.1 = bf16[512,2048]{0,1:T(8,128)(2,1)} fusion(bf16[512,2048]{0,1:T(8,128)(2,1)S(1)} %copy-done.3, bf16[2048,512]{1,0:T(8,128)(2,1)} %reduce-scatter.2.cloned.1.call-done, bf16[512,2048]{0,1:T(8,128)(2,1)} %copy.33, pred[512]{0:T(512)(128)(4,1)S(1)} %get-tuple-element.5), kind=kLoop, calls=%fused_computation.17 | loop fusion | flops 7340032 | bytes 8389120 | tf_op jit(solution)/shard_map/convert_element_type | solution.py:127
  281.7 1.3 collective-permute-start
  283.0 5.1 %collective-permute-done = bf16[512,2048]{0,1:T(8,128)(2,1)} collective-permute-done((bf16[512,2048]{0,1:T(8,128)(2,1)}, bf16[512,2048]{0,1:T(8,128)(2,1)}, u32[]{:S(2)}, u32[]{:S(2)}) %collective-permute-start) | collective-permute-done | bytes 2097184 | tf_op jit(solution)/shard_map/ppermute | solution.py:10
  288.1 0.0 copy-start.1
  288.1 5.6 %fusion.13 = bf16[1,512,2048]{1,2,0:T(8,128)(2,1)} fusion(bf16[2048,512]{1,0:T(8,128)(2,1)} %reduce-scatter.2.cloned.1.call-done, bf16[512,2048]{0,1:T(8,128)(2,1)} %copy.34, bf16[512,2048]{0,1:T(8,128)(2,1)} %collective-permute-done, pred[]{:T(512)S(6)} %eq.48, bf16[512,2048]{0,1:T(8,128)(2,1)} %copy.33, pred[512]{0:T(512)(128)(4,1)S(1)} %get-tuple-element.5), kind=kLoop, calls=%fused_computation.20 | loop fusion | flops 8388608 | bytes 10486273 | tf_op jit(solution)/shard_map/broadcast_in_dim | solution.py:130
  293.7 3.9 %copy.35 = bf16[1,512,2048]{2,1,0:T(8,128)(2,1)} copy(bf16[1,512,2048]{1,2,0:T(8,128)(2,1)} %fusion.13) | data formatting | bytes 4194304 | tf_op jit(solution)/shard_map/broadcast_in_dim | solution.py:130
  297.6 0.0 copy-done.1
  (10 shorter events, 0.1 us)
Async XLA Ops:
  6.5 12.9 %copy-start = (bf16[1,512,2048]{2,1,0:T(8,128)(2,1)S(1)}, bf16[1,512,2048]{2,1,0:T(8,128)(2,1)}, u32[]{:S(2)}) copy-start(bf16[1,512,2048]{2,1,0:T(8,128)(2,1)} %param.9) | copy-start | bytes 6291460
  15.8 13.5 %all-to-all-start = ((bf16[4,2,128]{2,1,0:T(2,128)(2,1)}), bf16[4,2,128]{2,1,0:T(2,128)(2,1)S(1)}, u32[]{:S(2)}, u32[]{:S(2)}) async-start(bf16[4,2,128]{2,1,0:T(2,128)(2,1)} %reshape.351), calls=%async_computation.1 | async-start | bytes 4096 | tf_op jit(solution)/shard_map/all_to_all | solution.py:98
  29.3 51.8 %all-to-all-start.1 = ((bf16[4,256,2048]{2,1,0:T(8,128)(2,1)}), bf16[4,256,2048]{2,1,0:T(8,128)(2,1)}, u32[]{:S(2)}, u32[]{:S(2)}) async-start(bf16[4,256,2048]{2,1,0:T(8,128)(2,1)} %select_select_fusion), calls=%async_computation.2 | async-start | bytes 8388608 | tf_op jit(solution)/shard_map/all_to_all | solution.py:97
  34.3 131.8 %all-reduce.2.cloned.1.call-start = ((), (), s32[]{:S(2)}) async-start(), calls=%async_computation.5 | async-start | bytes 262144 | tf_op jit(solution)/shard_map/psum | solution.py:106
  94.4 183.0 %reduce-scatter.2.cloned.1.call-start = ((), (), s32[]{:S(2)}) async-start(), calls=%async_computation.4 | async-start | bytes 10485760 | tf_op jit(solution)/shard_map/reduce_scatter | solution.py:72
  120.3 1.2 copy-start.4
  120.3 1.9 copy-start.5
  185.4 51.8 %all-to-all-start.2 = ((bf16[4,256,2048]{2,1,0:T(8,128)(2,1)}), bf16[4,256,2048]{2,1,0:T(8,128)(2,1)}, u32[]{:S(2)}, u32[]{:S(2)}) async-start(bf16[4,256,2048]{2,1,0:T(8,128)(2,1)} %bitcast.79), calls=%async_computation.3 | async-start | bytes 8388608 | tf_op jit(solution)/shard_map/all_to_all | solution.py:117
  190.3 4.1 %copy-start.2 = (s32[512]{0:T(512)S(1)}, s32[512]{0:T(512)}, u32[]{:S(2)}) copy-start(s32[512]{0:T(512)} %param.15) | copy-start | bytes 6148
  245.1 32.2 %copy-start.3 = (bf16[512,2048]{0,1:T(8,128)(2,1)S(1)}, bf16[512,2048]{0,1:T(8,128)(2,1)}, u32[]{:S(2)}) copy-start(bf16[512,2048]{0,1:T(8,128)(2,1)} %copy.34) | copy-start | bytes 6291460
  281.7 6.4 %collective-permute-start = (bf16[512,2048]{0,1:T(8,128)(2,1)}, bf16[512,2048]{0,1:T(8,128)(2,1)}, u32[]{:S(2)}, u32[]{:S(2)}) collective-permute-start(bf16[512,2048]{0,1:T(8,128)(2,1)} %add_convert_fusion.1), channel_id=1, source_target_pairs={{0,4},{1,5},{2,6},{3,7},{8,12},{9,13},{10,14},{11,15},{16,20},{17,... | collective-permute-start | bytes 6291464 | tf_op jit(solution)/shard_map/ppermute | solution.py:10
  288.1 9.5 %copy-start.1 = (bf16[1,512,2048]{2,1,0:T(8,128)(2,1)S(1)}, bf16[1,512,2048]{2,1,0:T(8,128)(2,1)}, u32[]{:S(2)}) copy-start(bf16[1,512,2048]{2,1,0:T(8,128)(2,1)} %param.9) | copy-start | bytes 6291460
Sparse Core Ops, SparseCore 0:
  94.5 33.0 all-reduce.1
  130.1 147.2 reduce-scatter.1
where the time goes:
time: 310 us; the launch traced here: 305 us
  waiting for transfers between devices  123 us (40%)
  matrix products  77.2 us (25%)
  local copies, waits for them, and re-layouts  40 us (13%)
  other arithmetic  36.2 us (12%)
  starting transfers between devices  14.8 us (5%)
  between operations  14 us (5%)
    all_to_all x1, waiting for transfers between devices, per_device(): lax.all_to_all(send_feat, 'pool', split_axis=0, concat_axis=0, tiled=True)  46.6 us
    all_to_all x1, waiting for transfers between devices, per_device(): lax.all_to_all(served.reshape(group_count, item_count, shard_width), 'poo...  42.7 us
    reduce_scatter x1, waiting for transfers between devices, per_device(): lax.psum_scatter(lax.dot_general(weight, features, (((0,), (1,)), ((), ()...  28.1 us
    dot_general x1, matrix products, per_device(): lax.dot_general(weight, features, (((0,), (1,)), ((), ())), preferred_ele...  25.7 us
    dot_general x1, matrix products, adapter_delta(): jnp.dot(spread, up_factor_rows.reshape(var_count * low_dim, shard_width),...  18.1 us
    dot_general x1, matrix products, adapter_delta(): block_sel = jnp.einsum('svj,sv->sj', block_y, select)  17.5 us
    dot_general x1, matrix products, adapter_delta(): lax.dot_general(features, down_factor_rows.reshape(var_count * low_dim, s...  13.2 us
    gather x2, local copies, waits for them, and re-layouts, per_device(): adapter_output = jnp.take(flat_back, owners * capacity + slot_pos, axis=0)  12 us
  transfers between devices with their start and end apart: 6, of which 4 were waited for; matrix products, arithmetic and copies ran while one was open for 38% of the time, Pallas kernels for 0%

commit v1 on v0

v1 whole, which is shorter than its diff:
```python
import functools
import math

import jax
import jax.numpy as jnp
from jax import lax
from jax.experimental import pallas as pl
from jax.experimental.pallas import tpu as pltpu
from jax.sharding import PartitionSpec as P

LANES = 128
LAG = 2
WINDOW = 3
BF16 = jnp.bfloat16
F32 = jnp.float32


def remote(src, dst, send_sem, recv_sem, **where):
    return pltpu.make_async_remote_copy(
        src_ref=src,
        dst_ref=dst,
        send_sem=send_sem,
        recv_sem=recv_sem,
        device_id=where,
        device_id_type=pl.DeviceIdType.MESH,
    )


def fused(
    cfg,
    feat, hidden, weight, down, up, mats, source, slot, var_send, place_tab,
    out,
    rbuf, wbuf, tmp, acc, sendf, recvf, retf, lowbuf, varbuf, comb, secbuf,
    lracc, lrp, pre_in, suf_in, pre_out, suf_out, yterm, placef, pickb,
    w_sem, low_sem, rs_send, rs_recv, a2a_send, a2a_recv, var_ssem, var_rsem,
    ret_send, ret_recv, lr_send, lr_recv, sec_send, sec_recv,
):
    n, pools, sections, rank, cw, tile = cfg
    rows, width = feat.shape
    groups = width // cw
    slots = recvf.shape[0]
    cap = slots // pools
    reps = LANES // rank
    low_rows = lowbuf.shape[0]
    i = lax.axis_index("tensor")
    me = lax.axis_index("pool")
    sec = lax.axis_index("section")
    seqs = (n - 1) * groups
    plus_at = (n - 1 - i) * groups + LAG * i
    minus_at = i * groups + LAG * (n - 1 - i)
    plus_first = (i > 0) & ((i == n - 1) | (plus_at <= minus_at))

    def low_copy(src):
        return pltpu.make_async_copy(src, lowbuf, low_sem)

    def parts(step, direction):
        lag_pos = i if direction == 0 else n - 1 - i
        seq = step - LAG * lag_pos
        valid = (seq >= 0) & (seq < seqs)
        seq = jnp.clip(seq, 0, seqs - 1)
        phase, chunk = seq // groups, seq % groups
        if direction == 0:
            target = n - 1 - phase
            sends = valid & (target > i)
            keeps = valid & (target == i)
            first = keeps & plus_first
            receives = i > 0
            index = target * groups + chunk
        else:
            target = phase
            sends = valid & (target < i)
            keeps = valid & (target == i)
            first = keeps & jnp.logical_not(plus_first)
            receives = i < n - 1
            index = jnp.where(target == i, n, target) * groups + chunk
        return seq, target, chunk, sends, keeps, first, receives, index

    def weight_copy(step, direction):
        _, target, chunk, _, _, _, _, _ = parts(step, direction)
        column = pl.multiple_of(target * width + chunk * cw, cw)
        return pltpu.make_async_copy(
            weight.at[:, pl.ds(column, cw)],
            wbuf.at[step % 2, direction],
            w_sem.at[step % 2, direction],
        )

    def fetch(step):
        for direction in range(2):
            _, _, _, sends, _, first, _, _ = parts(step, direction)

            @pl.when(sends | first)
            def _():
                weight_copy(step, direction).start()

    def rs_copy(direction, index):
        to = i + 1 if direction == 0 else i - 1
        return remote(
            rbuf.at[index], rbuf.at[index], rs_send.at[index], rs_recv.at[index],
            tensor=jnp.clip(to, 0, n - 1),
        )

    def rs_out(direction, seq):
        phase, chunk = seq // groups, seq % groups
        target = n - 1 - phase if direction == 0 else phase
        index = target * groups + chunk
        to = i + 1 if direction == 0 else i - 1
        landing = index
        if direction == 1:
            landing = jnp.where(target == to, n, target) * groups + chunk
        return remote(
            rbuf.at[index], rbuf.at[landing], rs_send.at[index], rs_recv.at[landing],
            tensor=jnp.clip(to, 0, n - 1),
        )

    def step_body(step):
        @pl.when(step + 1 < total_steps)
        def _():
            fetch(step + 1)

        for direction in range(2):
            seq, _, chunk, sends, keeps, first, receives, index = parts(step, direction)

            @pl.when(sends | first)
            def _():
                weight_copy(step, direction).wait()
                tmp[...] = jnp.dot(
                    feat[...], wbuf[step % 2, direction], preferred_element_type=F32
                )

            @pl.when((sends | keeps) & receives)
            def _():
                rs_copy(direction, index).wait_recv()

            @pl.when(sends)
            def _():
                @pl.when(receives)
                def _():
                    rbuf[index] = (tmp[...] + rbuf[index].astype(F32)).astype(BF16)

                @pl.when(jnp.logical_not(receives))
                def _():
                    rbuf[index] = tmp[...].astype(BF16)

                @pl.when(seq >= WINDOW)
                def _():
                    rs_out(direction, seq - WINDOW).wait_send()

                rs_out(direction, seq).start()

            @pl.when(first & receives)
            def _():
                acc[chunk] = tmp[...] + rbuf[index].astype(F32)

            @pl.when(first & jnp.logical_not(receives))
            def _():
                acc[chunk] = tmp[...]

            @pl.when(keeps & receives & jnp.logical_not(first))
            def _():
                acc[chunk] = acc[chunk] + rbuf[index].astype(F32)

    per_step = 2
    adapt_at = max(1, 3 * seqs // 8)
    hops_end = adapt_at + n - 1
    served_at = hops_end + pl.cdiv(groups, per_step)
    finals = [
        max((n - 1 - p) * groups + LAG * p, p * groups + LAG * (n - 1 - p), served_at)
        for p in range(n)
    ]
    total_steps = max(finals) + groups
    final_at = jnp.maximum(jnp.maximum(plus_at, minus_at), served_at)

    def sec_copy(chunk):
        cols = pl.ds(pl.multiple_of(chunk * cw, cw), cw)
        return remote(
            out.at[:, cols], secbuf.at[:, cols], sec_send.at[chunk], sec_recv.at[chunk],
            section=jnp.minimum(sec + 1, sections - 1),
        )

    def ret_copy(chunk, d):
        to = (me + d) % pools
        cols = pl.ds(pl.multiple_of(chunk * cw, cw), cw)
        return remote(
            recvf.at[pl.ds(pl.multiple_of(to * cap, cap), cap), cols],
            retf.at[pl.ds(pl.multiple_of(me * cap, cap), cap), cols],
            ret_send.at[chunk, to],
            ret_recv.at[chunk, me],
            pool=to,
        )

    def ret_arrival(chunk, d):
        owner = (me + d) % pools
        cols = pl.ds(pl.multiple_of(chunk * cw, cw), cw)
        return remote(
            recvf.at[pl.ds(pl.multiple_of(owner * cap, cap), cap), cols],
            retf.at[pl.ds(pl.multiple_of(owner * cap, cap), cap), cols],
            ret_send.at[chunk, owner],
            ret_recv.at[chunk, owner],
            pool=owner,
        )

    def finish(chunk):
        cols = pl.ds(pl.multiple_of(chunk * cw, cw), cw)
        for d in range(1, pools):
            ret_arrival(chunk, d).wait_recv()
        tmp[...] = acc[chunk] + jnp.dot(comb[...], retf[:, cols], preferred_element_type=F32)

        @pl.when(sec == 0)
        def _():
            out[:, cols] = (hidden[:, cols].astype(F32) + tmp[...]).astype(BF16)

        @pl.when(sec > 0)
        def _():
            sec_copy(chunk).wait_recv()
            out[:, cols] = (secbuf[:, cols].astype(F32) + tmp[...]).astype(BF16)

        @pl.when(sec < sections - 1)
        def _():
            sec_copy(chunk).start()

    def steps(first, last):
        @pl.loop(first, last)
        def _(step):
            step_body(step)
            chunk = step - final_at

            @pl.when((chunk >= 0) & (chunk < groups))
            def _():
                finish(chunk)

    def row_copy(d):
        to = (me + d) % pools
        return remote(
            sendf.at[pl.ds(pl.multiple_of(to * cap, cap), cap), pl.ds(0, width)],
            recvf.at[pl.ds(pl.multiple_of(me * cap, cap), cap)],
            a2a_send.at[to], a2a_recv.at[me], pool=to,
        )

    def var_copy(d):
        to = (me + d) % pools
        return remote(
            var_send.at[pl.ds(pl.multiple_of(to * cap, cap), cap)],
            varbuf.at[pl.ds(pl.multiple_of(me * cap, cap), cap)],
            var_ssem.at[to], var_rsem.at[me], pool=to,
        )

    def arrival(d):
        owner = (me + d) % pools
        block = pl.ds(pl.multiple_of(owner * cap, cap), cap)
        return (
            remote(sendf.at[block, pl.ds(0, width)], recvf.at[block], a2a_send.at[owner], a2a_recv.at[owner], pool=owner),
            remote(var_send.at[block], varbuf.at[block], var_ssem.at[owner], var_rsem.at[owner], pool=owner),
        )

    def pre_copy():
        return remote(pre_out, pre_in, lr_send.at[0], lr_recv.at[0],
                      tensor=jnp.minimum(i + 1, n - 1))

    def suf_copy():
        return remote(suf_out, suf_in, lr_send.at[1], lr_recv.at[1],
                      tensor=jnp.maximum(i - 1, 0))

    barrier = pltpu.get_barrier_semaphore()
    for d in range(1, pools):
        pl.semaphore_signal(barrier, inc=1, device_id={"pool": (me + d) % pools},
                            device_id_type=pl.DeviceIdType.MESH)
    for d in range(1, sections):
        pl.semaphore_signal(barrier, inc=1, device_id={"section": (sec + d) % sections},
                            device_id_type=pl.DeviceIdType.MESH)

    @pl.when(i > 0)
    def _():
        pl.semaphore_signal(barrier, inc=1, device_id={"tensor": jnp.maximum(i - 1, 0)},
                            device_id_type=pl.DeviceIdType.MESH)

    @pl.when(i < n - 1)
    def _():
        pl.semaphore_signal(barrier, inc=1, device_id={"tensor": jnp.minimum(i + 1, n - 1)},
                            device_id_type=pl.DeviceIdType.MESH)

    fetch(0)
    low_copy(down).start()
    pl.semaphore_wait(
        barrier,
        pools - 1 + sections - 1 + (i > 0).astype(jnp.int32) + (i < n - 1).astype(jnp.int32),
    )

    steps(0, 1)

    def dispatch(owner, into):
        block = pl.ds(pl.multiple_of(owner * cap, cap), cap)
        pick = (
            source[block, :] == lax.broadcasted_iota(jnp.int32, (cap, rows), 1)
        ).astype(F32).astype(BF16)

        @pl.loop(0, groups)
        def _(chunk):
            cols = pl.ds(pl.multiple_of(chunk * cw, cw), cw)
            into[block, cols] = jnp.dot(
                pick, feat[:, cols], preferred_element_type=F32
            ).astype(BF16)

    for d in range(1, pools):
        var_copy(d).start()

    @pl.loop(1, pools)
    def _(d):
        dispatch((me + d) % pools, sendf)
        row_copy(d).start()

    dispatch(me, recvf)
    own = pl.ds(pl.multiple_of(me * cap, cap), cap)
    varbuf[own, :] = var_send[own, :]
    comb[...] = (
        slot[...] == lax.broadcasted_iota(jnp.int32, (rows, slots), 1)
    ).astype(F32).astype(BF16)

    steps(1, adapt_at)

    for d in range(1, pools):
        rows_in, vars_in = arrival(d)
        rows_in.wait_recv()
        vars_in.wait_recv()
    low_copy(down).wait()
    lane = lax.broadcasted_iota(jnp.int32, (slots, LANES), 1)
    lane_var = (lane // rank).astype(F32)
    per_tile = tile // LANES
    lracc[...] = jnp.zeros_like(lracc)

    @pl.loop(0, low_rows // tile)
    def _(t):
        product = lax.dot_general(
            recvf[...], lowbuf[pl.ds(pl.multiple_of(t * tile, tile), tile), :],
            (((1,), (1,)), ((), ())), preferred_element_type=F32,
        )
        base_var = varbuf[...].astype(F32) - lane_var
        total = lracc[...]
        for b in range(per_tile):
            wanted = ((t * per_tile + b) * reps).astype(F32)
            total = total + jnp.where(
                base_var == wanted, product[:, b * LANES:(b + 1) * LANES], 0.0
            )
        lracc[...] = total

    low_copy(up).start()
    folded = lracc[...]
    for j in range(1, reps):
        folded = folded + pltpu.roll(lracc[...], j * rank, 1)
    packed_rows = slots // reps
    lane_p = lax.broadcasted_iota(jnp.int32, (packed_rows, LANES), 1) // rank
    packed = jnp.zeros((packed_rows, LANES), F32)
    for j in range(reps):
        packed = jnp.where(lane_p == j, folded[j * packed_rows:(j + 1) * packed_rows], packed)
    lrp[...] = packed

    def hop(h):
        @pl.when(i == h)
        def _():
            @pl.when(i > 0)
            def _():
                pre_copy().wait_recv()

            @pl.when(i == 0)
            def _():
                pre_out[...] = lrp[...].astype(BF16)

            @pl.when((i > 0) & (i < n - 1))
            def _():
                pre_out[...] = (lrp[...] + pre_in[...].astype(F32)).astype(BF16)

            @pl.when(i < n - 1)
            def _():
                pre_copy().start()

        @pl.when(n - 1 - i == h)
        def _():
            @pl.when(i < n - 1)
            def _():
                suf_copy().wait_recv()

            @pl.when(i == n - 1)
            def _():
                suf_out[...] = lrp[...].astype(BF16)

            @pl.when((i > 0) & (i < n - 1))
            def _():
                suf_out[...] = (lrp[...] + suf_in[...].astype(F32)).astype(BF16)

            @pl.when(i > 0)
            def _():
                suf_copy().start()

    hop(0)

    hot = (varbuf[...].astype(F32) == lane.astype(F32)).astype(F32).astype(BF16)
    placef[...] = jnp.dot(hot, place_tab[...], preferred_element_type=F32)
    yterm[...] = jnp.zeros_like(yterm)

    @pl.loop(0, width // LANES)
    def _(p):
        block = recvf[:, pl.ds(pl.multiple_of(p * LANES, LANES), LANES)].astype(F32)
        yterm[...] = jnp.where(placef[...] == p.astype(F32), block, yterm[...])

    pickb[...] = yterm[...]
    yterm[...] = jnp.zeros_like(yterm)
    bunch = math.gcd(4, mats.shape[0] // LANES)
    bunch_rows = bunch * LANES

    @pl.loop(0, mats.shape[0] // bunch_rows)
    def _(g):
        masked = [
            jnp.where(
                varbuf[...].astype(F32) == (g * bunch + b).astype(F32), pickb[...], 0.0
            ).astype(BF16)
            for b in range(bunch)
        ]
        yterm[...] += jnp.dot(
            jnp.concatenate(masked, axis=1),
            mats[pl.ds(pl.multiple_of(g * bunch_rows, bunch_rows), bunch_rows), :],
            preferred_element_type=F32,
        )

    @pl.loop(1, n)
    def _(h):
        steps(adapt_at + h - 1, adapt_at + h)
        hop(h)

    @pl.when(i > 0)
    def _():
        lrp[...] += pre_in[...].astype(F32)

    @pl.when(i < n - 1)
    def _():
        lrp[...] += suf_in[...].astype(F32)

    for d in range(1, pools):
        row_copy(d).wait_send()
        var_copy(d).wait_send()
    for j in range(reps):
        mine = jnp.where(lane_p == j, lrp[...], 0.0)
        spread = mine
        for k in range(1, reps):
            spread = spread + pltpu.roll(mine, k * rank, 1)
        spread = spread.astype(BF16)
        block = pl.ds(j * packed_rows, packed_rows)
        base_var = varbuf[block, :].astype(F32) - lane_p.astype(F32)
        for b in range(low_rows // LANES):
            sendf[block, b * LANES:(b + 1) * LANES] = jnp.where(
                base_var == float(b * reps), spread, 0.0
            ).astype(BF16)
    low_copy(up).wait()

    def serve(chunk):
        cols = pl.ds(pl.multiple_of(chunk * cw, cw), cw)
        answer = jnp.dot(sendf[:, 0:low_rows], lowbuf[:, cols], preferred_element_type=F32)
        placed = [
            jnp.where(placef[...] == (chunk * (cw // LANES) + b).astype(F32), yterm[...], 0.0)
            for b in range(cw // LANES)
        ]
        recvf[:, cols] = (answer + jnp.concatenate(placed, axis=1)).astype(BF16)
        for d in range(1, pools):
            ret_copy(chunk, d).start()
        retf[own, cols] = recvf[own, cols]

    per_step = 2
    @pl.loop(0, groups)
    def _(chunk):
        serve(chunk)

        @pl.when(chunk % per_step == per_step - 1)
        def _():
            at = hops_end + chunk // per_step
            steps(at, at + 1)

    steps(hops_end + groups // per_step, total_steps)

    for direction in range(2):
        count = ((n - 1 - i) if direction == 0 else i) * groups

        @pl.loop(jnp.maximum(count - WINDOW, 0), count)
        def _(seq):
            rs_out(direction, seq).wait_send()

    @pl.when(i < n - 1)
    def _():
        pre_copy().wait_send()

    @pl.when(i > 0)
    def _():
        suf_copy().wait_send()

    @pl.loop(0, groups)
    def _(chunk):
        for d in range(1, pools):
            ret_copy(chunk, d).wait_send()

        @pl.when(sec < sections - 1)
        def _():
            sec_copy(chunk).wait_send()


def per_device(
    mesh,
    hidden_input,
    attention_output,
    projection_weight,
    lowrank_down_factor,
    lowrank_up_factor,
    residual_block_mats,
    diagonal_block_index,
    row_variant_index,
):
    n, pools, sections = mesh.shape["tensor"], mesh.shape["pool"], mesh.shape["section"]
    feat, weight = attention_output[0], projection_weight[0]
    down, up, mats = lowrank_down_factor[0], lowrank_up_factor[0], residual_block_mats[0][:, 0]
    rows, width = feat.shape
    variants, rank, _ = down.shape
    block = mats.shape[-1]
    low_rows = variants * rank
    cap = rows // 2
    slots = pools * cap
    cw = min(256, width)
    groups = width // cw
    tile = min(256, low_rows)
    reps = LANES // rank
    per_shard = width // block

    owners = row_variant_index // variants
    owner_hot = (owners[:, None] == jnp.arange(pools)[None, :]).astype(jnp.int32)
    counts = jnp.sum(owner_hot, axis=0)
    starts = jnp.cumsum(counts) - counts
    position = jnp.arange(rows) - jnp.sum(owner_hot * starts[None, :], axis=1)
    slot = (owners * cap + position).astype(jnp.int32)[:, None]
    places = jnp.arange(cap)[None, :]
    filled = places < counts[:, None]
    source = jnp.where(filled, starts[:, None] + places, -1).astype(jnp.int32)
    taken = jnp.take(row_variant_index, jnp.maximum(source, 0))
    var_send = jnp.where(filled, taken - jnp.arange(pools)[:, None] * variants, -1)
    var_send = jnp.broadcast_to(
        var_send.reshape(slots, 1).astype(BF16), (slots, LANES)
    )
    place = diagonal_block_index[0][:, 0] - lax.axis_index("tensor") * per_shard
    place_tab = jnp.zeros((LANES, LANES), BF16).at[:variants].set(
        jnp.broadcast_to(place.astype(BF16)[:, None], (variants, LANES))
    )

    vmem = pl.BlockSpec(memory_space=pltpu.VMEM)
    hbm = pl.BlockSpec(memory_space=pl.ANY)
    packed = (slots // reps, LANES)
    dma = pltpu.SemaphoreType.DMA
    out = pl.pallas_call(
        functools.partial(fused, (n, pools, sections, rank, cw, tile)),
        out_shape=jax.ShapeDtypeStruct((rows, width), BF16),
        in_specs=[vmem, vmem, hbm, hbm, hbm, vmem, vmem, vmem, vmem, vmem],
        out_specs=vmem,
        scratch_shapes=[
            pltpu.VMEM(((n + 1) * groups, rows, cw), BF16),
            pltpu.VMEM((2, 2, width, cw), BF16),
            pltpu.VMEM((rows, cw), F32),
            pltpu.VMEM((groups, rows, cw), F32),
            pltpu.VMEM((slots, max(width, low_rows)), BF16),
            pltpu.VMEM((slots, width), BF16),
            pltpu.VMEM((slots, width), BF16),
            pltpu.VMEM((low_rows, width), BF16),
            pltpu.VMEM((slots, LANES), BF16),
            pltpu.VMEM((rows, slots), BF16),
            pltpu.VMEM((rows, width), BF16),
            pltpu.VMEM((slots, LANES), F32),
            pltpu.VMEM(packed, F32),
            pltpu.VMEM(packed, BF16),
            pltpu.VMEM(packed, BF16),
            pltpu.VMEM(packed, BF16),
            pltpu.VMEM(packed, BF16),
            pltpu.VMEM((slots, LANES), F32),
            pltpu.VMEM((slots, LANES), F32),
            pltpu.VMEM((slots, LANES), F32),
            dma((2, 2)),
            dma,
            dma(((n + 1) * groups,)),
            dma(((n + 1) * groups,)),
            dma((pools,)),
            dma((pools,)),
            dma((pools,)),
            dma((pools,)),
            dma((groups, pools)),
            dma((groups, pools)),
            dma((2,)),
            dma((2,)),
            dma((groups,)),
            dma((groups,)),
        ],
        compiler_params=pltpu.CompilerParams(
            collective_id=0, has_side_effects=True, vmem_limit_bytes=60 * 1024 * 1024
        ),
        cost_estimate=pl.CostEstimate(
            flops=2 * rows * width * width * n + 4 * slots * low_rows * width,
            bytes_accessed=2 * (width * width * n + 2 * low_rows * width),
            transcendentals=0,
        ),
    )(
        feat, hidden_input, weight, down.reshape(low_rows, width), up.reshape(low_rows, width),
        mats.reshape(variants * block, block), source.reshape(slots, 1), slot, var_send, place_tab,
    )
    return out[None]


def solution(mesh):
    return jax.shard_map(
        functools.partial(per_device, mesh),
        mesh=mesh,
        in_specs=(
            P("pool", "tensor"),
            P("section", "pool", "tensor"),
            P("section", "tensor", None),
            P("section", "pool", None, "tensor"),
            P("section", "pool", None, "tensor"),
            P("section", "pool", "tensor", None, None),
            P("section", "pool", "tensor"),
            P("pool"),
        ),
        out_specs=P("section", "pool", "tensor"),
        check_vma=False,
    )
```

time: 310 us -> 186 us (0.60); the launches traced: 305 us -> 185 us
  Pallas kernels: 0 us -> 169 us
  waiting for transfers between devices: 123 us -> 0 us
  matrix products: 77.2 us -> 0 us
  other arithmetic: 36.2 us -> 2.62 us
  local copies, waits for them, and re-layouts: 40 us -> 13.6 us
  starting transfers between devices: 14.8 us -> 0 us
  between operations: 14 us -> 0.08 us
    pallas_call x0 -> x1, Pallas kernels: none -> 169 us  [per_device(): pl.pallas_call(functools.partial(fused, (n, pools, sections, rank, cw, ti...]
    all_to_all x3 -> x0, waiting for transfers between devices: 89.3 us -> none  [the longest x1 46.6 us: per_device(): lax.all_to_all(send_feat, 'pool', split_axis=0, concat_axis=0, tiled=True)]
    dot_general x6 -> x0, matrix products: 77.2 us -> none  [the longest x1 25.7 us: per_device(): lax.dot_general(weight, features, (((0,), (1,)), ((), ())), preferred_ele...]
    reduce_scatter x1 -> x0, waiting for transfers between devices: 28.1 us -> none  [per_device(): lax.psum_scatter(lax.dot_general(weight, features, (((0,), (1,)), ((), ()...]
    gather x4 -> x1, local copies, waits for them, and re-layouts: 24.2 us -> 6.87 us  [per_device(): taken = jnp.take(row_variant_index, jnp.maximum(source, 0))]
    all_to_all x3 -> x0, starting transfers between devices: 13.3 us -> none  [the longest x1 4.94 us: per_device(): lax.all_to_all(send_feat, 'pool', split_axis=0, concat_axis=0, tiled=True)]
    reduce_sum x2 -> x1, other arithmetic: 11.7 us -> 0.09 us  [per_device(): position = jnp.arange(rows) - jnp.sum(owner_hot * starts[None, :], axis=1)]
    mul x2 -> x1, other arithmetic: 8.4 us -> 0.01 us  [per_device(): jnp.arange(pools)[:, None] * variants]
  transfers between devices with their start and end apart: 6 -> 0, of which waited for: 4 -> 0; matrix products, arithmetic and copies ran while one was open for 38% -> 0% of each run, Pallas kernels for 0% -> 0%
where the time goes in v1:
time: 186 us; the launch traced here: 185 us
  Pallas kernels  169 us (91%)
  local copies, waits for them, and re-layouts  13.6 us (7%)
  other arithmetic  2.62 us (1%)
    pallas_call x1, Pallas kernels, per_device(): pl.pallas_call(functools.partial(fused, (n, pools, sections, rank, cw, ti...  169 us
    gather x1, local copies, waits for them, and re-layouts, per_device(): taken = jnp.take(row_variant_index, jnp.maximum(source, 0))  6.87 us
    unnamed x14, local copies, waits for them, and re-layouts  4.3 us

profile of v1, /device:TPU:17, one launch (start us, length us, event | category | flops | bytes accessed | tf_op | source)
XLA Modules:
  0.0 185.2 jit_solution(14581694670280549499)
XLA Ops:
  0.0 0.0 copy-start
  0.0 0.7 convert_bitcast_fusion
  0.7 0.7 add_select_fusion
  1.4 0.1 convert_reduce_fusion
  1.5 0.2 reduce-window.7
  1.7 0.1 select_reduce_fusion
  1.8 0.7 subtract_add_fusion
  2.5 0.1 broadcast_bitcast_fusion
  2.5 0.1 maximum_bitcast_fusion
  2.6 0.0 copy-done
  2.6 6.9 %gather_fusion = s32[1024]{0:T(1024)S(1)} fusion(s32[512]{0:T(512)S(1)} %copy-done, s32[1024]{0:T(1024)S(1)} %broadcast_clamp_fusion), kind=kCustom, calls=%fused_computation | custom fusion | bytes 12288 | tf_op jit(solution)/shard_map/jit(_take)/gather | solution.py:537
  9.6 0.1 broadcast_bitcast_fusion.2
  9.7 0.7 scatter.8.place_tab
  10.4 0.9 broadcast_in_dim.43.var_send
  11.3 0.9 copy.12.slot
  12.1 1.0 copy.14
  13.2 168.9 %shard_map.82 = bf16[512,2048]{1,0:T(8,128)(2,1)} custom-call(bf16[512,2048]{1,0:T(8,128)(2,1)} %bitcast.51, bf16[512,2048]{1,0:T(8,128)(2,1)} %hidden.1, bf16[2048,8192]{1,0:T(8,128)(2,1)} %bitcast.48, bf16[2048,2048]{1,0:T(8,128)(2,1)} %bitcast.49, bf16[2048,2048]{1,0:T(8,128)(2,1)} %bitcast.50, bf16[4096,128]{1,0:T(8,128)(2,1)} %bitcast.52, ...), custom_call_target="tpu_custom_call" | custom-call | flops 34359738368 | bytes 50331648 | tf_op jit(solution)/shard_map/pallas_call | solution.py:551
  182.1 3.2 %copy.22 = bf16[1,512,2048]{2,1,0:T(8,128)(2,1)} copy(bf16[1,512,2048]{2,1,0:T(8,128)(2,1)} %bitcast.37) | data formatting | bytes 4194304
  (14 shorter events, 0.1 us)
Async XLA Ops:
  0.0 2.6 %copy-start = (s32[512]{0:T(512)S(1)}, s32[512]{0:T(512)}, u32[]{:S(2)}) copy-start(s32[512]{0:T(512)} %param.17) | copy-start | bytes 6148

commit v2 on v1

--- a/solution.py
+++ b/solution.py
@@ -10,7 +10,7 @@
 
 LANES = 128
 LAG = 2
-WINDOW = 3
+WINDOW = 4
 BF16 = jnp.bfloat16
 F32 = jnp.float32
 
@@ -28,10 +28,10 @@
 
 def fused(
     cfg,
-    feat, hidden, weight, down, up, mats, source, slot, var_send, place_tab,
+    feat, hidden, weight, down, up, mats, row_var, place_of,
     out,
     rbuf, wbuf, tmp, acc, sendf, recvf, retf, lowbuf, varbuf, comb, secbuf,
-    lracc, lrp, pre_in, suf_in, pre_out, suf_out, yterm, placef, pickb,
+    lracc, lrp, pre_in, suf_in, pre_out, suf_out, yterm, placef, pickb, var_send,
     w_sem, low_sem, rs_send, rs_recv, a2a_send, a2a_recv, var_ssem, var_rsem,
     ret_send, ret_recv, lr_send, lr_recv, sec_send, sec_recv,
 ):
@@ -160,9 +160,11 @@
                 acc[chunk] = acc[chunk] + rbuf[index].astype(F32)
 
     per_step = 2
-    adapt_at = max(1, 3 * seqs // 8)
-    hops_end = adapt_at + n - 1
-    served_at = hops_end + pl.cdiv(groups, per_step)
+    tiles = low_rows // tile
+    tiles_per_step = 3
+    adapt_at = max(3, 5 * seqs // 12)
+    hops_at = adapt_at + tiles // tiles_per_step
+    served_at = hops_at + max(n - 1, 2)
     finals = [
         max((n - 1 - p) * groups + LAG * p, p * groups + LAG * (n - 1 - p), served_at)
         for p in range(n)
@@ -285,13 +287,30 @@
         pools - 1 + sections - 1 + (i > 0).astype(jnp.int32) + (i < n - 1).astype(jnp.int32),
     )
 
-    steps(0, 1)
-
-    def dispatch(owner, into):
+    steps(0, 2)
+
+    variants = low_rows // rank
+    ids = row_var[...]
+    place_in_block = lax.broadcasted_iota(jnp.int32, (1, rows), 1)
+
+    def picks_of(owner):
+        mine = (ids >= owner * variants) & (ids < (owner + 1) * variants)
+        start = jnp.sum((ids < owner * variants).astype(F32), axis=1, keepdims=True)
+        position = jnp.where(mine, place_in_block.astype(F32) - start, -1.0)
+        slot = lax.broadcasted_iota(jnp.int32, (cap, rows), 0).astype(F32)
+        return (slot == position).astype(F32)
+
+    def dispatch(owner, into, vars_into):
         block = pl.ds(pl.multiple_of(owner * cap, cap), cap)
-        pick = (
-            source[block, :] == lax.broadcasted_iota(jnp.int32, (cap, rows), 1)
-        ).astype(F32).astype(BF16)
+        pick = picks_of(owner).astype(BF16)
+        local = (ids - owner * variants + 1).astype(F32).astype(BF16)
+        vars_into[block, :] = (
+            lax.dot_general(
+                pick, jnp.broadcast_to(local, (LANES, rows)),
+                (((1,), (1,)), ((), ())), preferred_element_type=F32,
+            )
+            - 1.0
+        ).astype(BF16)
 
         @pl.loop(0, groups)
         def _(chunk):
@@ -300,22 +319,19 @@
                 pick, feat[:, cols], preferred_element_type=F32
             ).astype(BF16)
 
-    for d in range(1, pools):
-        var_copy(d).start()
-
     @pl.loop(1, pools)
     def _(d):
-        dispatch((me + d) % pools, sendf)
+        dispatch((me + d) % pools, sendf, var_send)
         row_copy(d).start()
-
-    dispatch(me, recvf)
+        var_copy(d).start()
+
+    steps(2, 3)
     own = pl.ds(pl.multiple_of(me * cap, cap), cap)
-    varbuf[own, :] = var_send[own, :]
-    comb[...] = (
-        slot[...] == lax.broadcasted_iota(jnp.int32, (rows, slots), 1)
-    ).astype(F32).astype(BF16)
-
-    steps(1, adapt_at)
+    dispatch(me, recvf, varbuf)
+    for q in range(pools):
+        comb[:, q * cap:(q + 1) * cap] = picks_of(q).T.astype(BF16)
+
+    steps(3, adapt_at)
 
     for d in range(1, pools):
         rows_in, vars_in = arrival(d)
@@ -327,7 +343,7 @@
     per_tile = tile // LANES
     lracc[...] = jnp.zeros_like(lracc)
 
-    @pl.loop(0, low_rows // tile)
+    @pl.loop(0, tiles)
     def _(t):
         product = lax.dot_general(
             recvf[...], lowbuf[pl.ds(pl.multiple_of(t * tile, tile), tile), :],
@@ -341,6 +357,11 @@
                 base_var == wanted, product[:, b * LANES:(b + 1) * LANES], 0.0
             )
         lracc[...] = total
+
+        @pl.when(t % tiles_per_step == tiles_per_step - 1)
+        def _():
+            at = adapt_at + t // tiles_per_step
+            steps(at, at + 1)
 
     low_copy(up).start()
     folded = lracc[...]
@@ -392,8 +413,16 @@
 
     hop(0)
 
-    hot = (varbuf[...].astype(F32) == lane.astype(F32)).astype(F32).astype(BF16)
-    placef[...] = jnp.dot(hot, place_tab[...], preferred_element_type=F32)
+    steps(hops_at, hops_at + 1)
+    hop(1)
+
+    lane_v = lax.broadcasted_iota(jnp.int32, (slots, variants), 1).astype(F32)
+    hot = (varbuf[:, 0:variants].astype(F32) == lane_v).astype(F32).astype(BF16)
+    place = (place_of[...] - i * (width // LANES)).astype(F32).astype(BF16)
+    placef[...] = lax.dot_general(
+        hot, jnp.broadcast_to(place, (LANES, variants)),
+        (((1,), (1,)), ((), ())), preferred_element_type=F32,
+    )
     yterm[...] = jnp.zeros_like(yterm)
 
     @pl.loop(0, width // LANES)
@@ -402,6 +431,8 @@
         yterm[...] = jnp.where(placef[...] == p.astype(F32), block, yterm[...])
 
     pickb[...] = yterm[...]
+    steps(hops_at + 1, hops_at + 2)
+    hop(2)
     yterm[...] = jnp.zeros_like(yterm)
     bunch = math.gcd(4, mats.shape[0] // LANES)
     bunch_rows = bunch * LANES
@@ -420,9 +451,9 @@
             preferred_element_type=F32,
         )
 
-    @pl.loop(1, n)
+    @pl.loop(3, max(n, 3))
     def _(h):
-        steps(adapt_at + h - 1, adapt_at + h)
+        steps(hops_at + h - 1, hops_at + h)
         hop(h)
 
     @pl.when(i > 0)
@@ -469,10 +500,10 @@
 
         @pl.when(chunk % per_step == per_step - 1)
         def _():
-            at = hops_end + chunk // per_step
+            at = served_at + chunk // per_step
             steps(at, at + 1)
 
-    steps(hops_end + groups // per_step, total_steps)
+    steps(served_at + groups // per_step, total_steps)
 
     for direction in range(2):
         count = ((n - 1 - i) if direction == 0 else i) * groups
@@ -523,26 +554,6 @@
     groups = width // cw
     tile = min(256, low_rows)
     reps = LANES // rank
-    per_shard = width // block
-
-    owners = row_variant_index // variants
-    owner_hot = (owners[:, None] == jnp.arange(pools)[None, :]).astype(jnp.int32)
-    counts = jnp.sum(owner_hot, axis=0)
-    starts = jnp.cumsum(counts) - counts
-    position = jnp.arange(rows) - jnp.sum(owner_hot * starts[None, :], axis=1)
-    slot = (owners * cap + position).astype(jnp.int32)[:, None]
-    places = jnp.arange(cap)[None, :]
-    filled = places < counts[:, None]
-    source = jnp.where(filled, starts[:, None] + places, -1).astype(jnp.int32)
-    taken = jnp.take(row_variant_index, jnp.maximum(source, 0))
-    var_send = jnp.where(filled, taken - jnp.arange(pools)[:, None] * variants, -1)
-    var_send = jnp.broadcast_to(
-        var_send.reshape(slots, 1).astype(BF16), (slots, LANES)
-    )
-    place = diagonal_block_index[0][:, 0] - lax.axis_index("tensor") * per_shard
-    place_tab = jnp.zeros((LANES, LANES), BF16).at[:variants].set(
-        jnp.broadcast_to(place.astype(BF16)[:, None], (variants, LANES))
-    )
 
     vmem = pl.BlockSpec(memory_space=pltpu.VMEM)
     hbm = pl.BlockSpec(memory_space=pl.ANY)
@@ -551,7 +562,7 @@
     out = pl.pallas_call(
         functools.partial(fused, (n, pools, sections, rank, cw, tile)),
         out_shape=jax.ShapeDtypeStruct((rows, width), BF16),
-        in_specs=[vmem, vmem, hbm, hbm, hbm, vmem, vmem, vmem, vmem, vmem],
+        in_specs=[vmem, vmem, hbm, hbm, hbm, vmem, vmem, vmem],
         out_specs=vmem,
         scratch_shapes=[
             pltpu.VMEM(((n + 1) * groups, rows, cw), BF16),
@@ -574,6 +585,7 @@
             pltpu.VMEM((slots, LANES), F32),
             pltpu.VMEM((slots, LANES), F32),
             pltpu.VMEM((slots, LANES), F32),
+            pltpu.VMEM((slots, LANES), BF16),
             dma((2, 2)),
             dma,
             dma(((n + 1) * groups,)),
@@ -599,7 +611,8 @@
         ),
     )(
         feat, hidden_input, weight, down.reshape(low_rows, width), up.reshape(low_rows, width),
-        mats.reshape(variants * block, block), source.reshape(slots, 1), slot, var_send, place_tab,
+        mats.reshape(variants * block, block), row_variant_index.reshape(1, rows),
+        diagonal_block_index[0].reshape(1, variants),
     )
     return out[None]
 

time: 186 us -> 161 us (0.87)
  Pallas kernels: 169 us -> 157 us
  local copies, waits for them, and re-layouts: 13.6 us -> 3.16 us
  other arithmetic: 2.62 us -> 0 us
    pallas_call x1, Pallas kernels: 169 us -> 157 us  [per_device(): pl.pallas_call(functools.partial(fused, (n, pools, sections, rank, cw, ti...]
    gather x1 -> x0, local copies, waits for them, and re-layouts: 6.87 us -> none  [per_device(): taken = jnp.take(row_variant_index, jnp.maximum(source, 0))]
    unnamed x14 -> x1, local copies, waits for them, and re-layouts: 4.3 us -> 3.16 us
where the time goes in v2:
time: 161 us; the launch traced here: 160 us
  Pallas kernels  157 us (98%)
  local copies, waits for them, and re-layouts  3.16 us (2%)
    pallas_call x1, Pallas kernels, per_device(): pl.pallas_call(functools.partial(fused, (n, pools, sections, rank, cw, ti...  157 us

profile of v2, /device:TPU:17, one launch (start us, length us, event | category | flops | bytes accessed | tf_op | source)
XLA Modules:
  0.0 160.1 jit_solution(12319099599207671982)
XLA Ops:
  0.0 156.9 %shard_map.82 = bf16[512,2048]{1,0:T(8,128)(2,1)} custom-call(bf16[512,2048]{1,0:T(8,128)(2,1)} %bitcast.12, bf16[512,2048]{1,0:T(8,128)(2,1)} %hidden.1, bf16[2048,8192]{1,0:T(8,128)(2,1)} %bitcast.9, bf16[2048,2048]{1,0:T(8,128)(2,1)} %bitcast.10, bf16[2048,2048]{1,0:T(8,128)(2,1)} %bitcast.11, bf16[4096,128]{1,0:T(8,128)(2,1)} %bitcast.13, ...), custom_call_target="tpu_custom_call" | custom-call | flops 34359738368 | bytes 50331648 | tf_op jit(solution)/shard_map/pallas_call | solution.py:562
  156.9 3.2 %copy.10 = bf16[1,512,2048]{2,1,0:T(8,128)(2,1)} copy(bf16[1,512,2048]{2,1,0:T(8,128)(2,1)} %bitcast.8) | data formatting | bytes 4194304

commit v3 on v2

--- a/solution.py
+++ b/solution.py
@@ -11,6 +11,7 @@
 LANES = 128
 LAG = 2
 WINDOW = 4
+NEAR_WINDOW = 2
 BF16 = jnp.bfloat16
 F32 = jnp.float32
 
@@ -28,12 +29,13 @@
 
 def fused(
     cfg,
-    feat, hidden, weight, down, up, mats, row_var, place_of,
-    out,
+    feat_in, hidden_in, weight, down, up, mats_in, row_var, place_of,
+    out_hbm,
+    feat, hidden, mats, out,
     rbuf, wbuf, tmp, acc, sendf, recvf, retf, lowbuf, varbuf, comb, secbuf,
     lracc, lrp, pre_in, suf_in, pre_out, suf_out, yterm, placef, pickb, var_send,
     w_sem, low_sem, rs_send, rs_recv, a2a_send, a2a_recv, var_ssem, var_rsem,
-    ret_send, ret_recv, lr_send, lr_recv, sec_send, sec_recv,
+    ret_send, ret_recv, lr_send, lr_recv, sec_send, sec_recv, in_sem, out_sem,
 ):
     n, pools, sections, rank, cw, tile = cfg
     rows, width = feat.shape
@@ -112,6 +114,10 @@
             tensor=jnp.clip(to, 0, n - 1),
         )
 
+    def left_by(seq):
+        near = jnp.where(seq >= adapt_at, jnp.minimum(seq, served_at) - NEAR_WINDOW, 0)
+        return jnp.maximum(jnp.maximum(seq - WINDOW, near), 0)
+
     def step_body(step):
         @pl.when(step + 1 < total_steps)
         def _():
@@ -141,9 +147,9 @@
                 def _():
                     rbuf[index] = tmp[...].astype(BF16)
 
-                @pl.when(seq >= WINDOW)
-                def _():
-                    rs_out(direction, seq - WINDOW).wait_send()
+                @pl.loop(left_by(seq - 1), left_by(seq))
+                def _(earlier):
+                    rs_out(direction, earlier).wait_send()
 
                 rs_out(direction, seq).start()
 
@@ -162,9 +168,9 @@
     per_step = 2
     tiles = low_rows // tile
     tiles_per_step = 3
-    adapt_at = max(3, 5 * seqs // 12)
+    adapt_at = max(3, 3 * seqs // 8)
     hops_at = adapt_at + tiles // tiles_per_step
-    served_at = hops_at + max(n - 1, 2)
+    served_at = hops_at + max(n - 2, 1)
     finals = [
         max((n - 1 - p) * groups + LAG * p, p * groups + LAG * (n - 1 - p), served_at)
         for p in range(n)
@@ -201,6 +207,10 @@
             pool=owner,
         )
 
+    def out_copy(chunk):
+        cols = pl.ds(pl.multiple_of(chunk * cw, cw), cw)
+        return pltpu.make_async_copy(out.at[:, cols], out_hbm.at[:, cols], out_sem.at[chunk])
+
     def finish(chunk):
         cols = pl.ds(pl.multiple_of(chunk * cw, cw), cw)
         for d in range(1, pools):
@@ -219,6 +229,8 @@
         @pl.when(sec < sections - 1)
         def _():
             sec_copy(chunk).start()
+
+        out_copy(chunk).start()
 
     def steps(first, last):
         @pl.loop(first, last)
@@ -280,13 +292,22 @@
         pl.semaphore_signal(barrier, inc=1, device_id={"tensor": jnp.minimum(i + 1, n - 1)},
                             device_id_type=pl.DeviceIdType.MESH)
 
+    feat_load = pltpu.make_async_copy(feat_in, feat, in_sem.at[0])
+    hidden_load = pltpu.make_async_copy(hidden_in, hidden, in_sem.at[1])
+    mats_load = pltpu.make_async_copy(mats_in, mats, in_sem.at[2])
+    feat_load.start()
     fetch(0)
+    mats_load.start()
+    hidden_load.start()
     low_copy(down).start()
     pl.semaphore_wait(
         barrier,
         pools - 1 + sections - 1 + (i > 0).astype(jnp.int32) + (i < n - 1).astype(jnp.int32),
     )
 
+    feat_load.wait()
+    mats_load.wait()
+    hidden_load.wait()
     steps(0, 2)
 
     variants = low_rows // rank
@@ -413,9 +434,6 @@
 
     hop(0)
 
-    steps(hops_at, hops_at + 1)
-    hop(1)
-
     lane_v = lax.broadcasted_iota(jnp.int32, (slots, variants), 1).astype(F32)
     hot = (varbuf[:, 0:variants].astype(F32) == lane_v).astype(F32).astype(BF16)
     place = (place_of[...] - i * (width // LANES)).astype(F32).astype(BF16)
@@ -431,8 +449,8 @@
         yterm[...] = jnp.where(placef[...] == p.astype(F32), block, yterm[...])
 
     pickb[...] = yterm[...]
-    steps(hops_at + 1, hops_at + 2)
-    hop(2)
+    hop(1)
+    steps(hops_at, hops_at + 1)
     yterm[...] = jnp.zeros_like(yterm)
     bunch = math.gcd(4, mats.shape[0] // LANES)
     bunch_rows = bunch * LANES
@@ -451,9 +469,11 @@
             preferred_element_type=F32,
         )
 
+    hop(2)
+
     @pl.loop(3, max(n, 3))
     def _(h):
-        steps(hops_at + h - 1, hops_at + h)
+        steps(hops_at + h - 2, hops_at + h - 1)
         hop(h)
 
     @pl.when(i > 0)
@@ -508,7 +528,7 @@
     for direction in range(2):
         count = ((n - 1 - i) if direction == 0 else i) * groups
 
-        @pl.loop(jnp.maximum(count - WINDOW, 0), count)
+        @pl.loop(left_by(count - 1), count)
         def _(seq):
             rs_out(direction, seq).wait_send()
 
@@ -528,6 +548,8 @@
         @pl.when(sec < sections - 1)
         def _():
             sec_copy(chunk).wait_send()
+
+        out_copy(chunk).wait()
 
 
 def per_device(
@@ -562,9 +584,13 @@
     out = pl.pallas_call(
         functools.partial(fused, (n, pools, sections, rank, cw, tile)),
         out_shape=jax.ShapeDtypeStruct((rows, width), BF16),
-        in_specs=[vmem, vmem, hbm, hbm, hbm, vmem, vmem, vmem],
-        out_specs=vmem,
+        in_specs=[hbm, hbm, hbm, hbm, hbm, hbm, vmem, vmem],
+        out_specs=hbm,
         scratch_shapes=[
+            pltpu.VMEM((rows, width), BF16),
+            pltpu.VMEM((rows, width), BF16),
+            pltpu.VMEM((variants * block, block), BF16),
+            pltpu.VMEM((rows, width), BF16),
             pltpu.VMEM(((n + 1) * groups, rows, cw), BF16),
             pltpu.VMEM((2, 2, width, cw), BF16),
             pltpu.VMEM((rows, cw), F32),
@@ -600,6 +626,8 @@
             dma((2,)),
             dma((groups,)),
             dma((groups,)),
+            dma((3,)),
+            dma((groups,)),
         ],
         compiler_params=pltpu.CompilerParams(
             collective_id=0, has_side_effects=True, vmem_limit_bytes=60 * 1024 * 1024

time: 161 us -> 170 us (1.056)
  Pallas kernels: 157 us -> 167 us
    pallas_call x1, Pallas kernels: 157 us -> 167 us  [per_device(): pl.pallas_call(functools.partial(fused, (n, pools, sections, rank, cw, ti...]
where the time goes in v3:
time: 170 us
  Pallas kernels  167 us (98%)
  local copies, waits for them, and re-layouts  3.16 us (2%)
    pallas_call x1, Pallas kernels, per_device(): pl.pallas_call(functools.partial(fused, (n, pools, sections, rank, cw, ti...  167 us

profile of v3, /device:TPU:17, one launch (start us, length us, event | category | flops | bytes accessed | tf_op | source)
XLA Modules:
  0.0 170.1 jit_solution(10384834244389617963)
XLA Ops:
  0.0 166.9 %shard_map.82 = bf16[512,2048]{1,0:T(8,128)(2,1)} custom-call(bf16[512,2048]{1,0:T(8,128)(2,1)} %bitcast.12, bf16[512,2048]{1,0:T(8,128)(2,1)} %hidden_in.1, bf16[2048,8192]{1,0:T(8,128)(2,1)} %bitcast.9, bf16[2048,2048]{1,0:T(8,128)(2,1)} %bitcast.10, bf16[2048,2048]{1,0:T(8,128)(2,1)} %bitcast.11, bf16[4096,128]{1,0:T(8,128)(2,1)} %bitcast.13, ...), custom_call_target="tpu_custom_call" | custom-call | flops 34359738368 | bytes 50331648 | tf_op jit(solution)/shard_map/pallas_call | solution.py:584
  166.9 3.2 %copy.10 = bf16[1,512,2048]{2,1,0:T(8,128)(2,1)} copy(bf16[1,512,2048]{2,1,0:T(8,128)(2,1)} %bitcast.8) | data formatting | bytes 4194304
